TPU v7x, 256 devices: a whole 4x4x8 slice. The times are simulated.
256 devices in a mesh: dp: 32 (over x, z_hi, core), fisher: 8 (over z_lo, y).
Axes of the slice: x: 4, y: 4, z: 8 (z_hi: 4, z_lo: 2; z = z_hi * 2 + z_lo), core: 2. Of those that a mesh axis runs over, the one named last changes fastest.
Arguments:
- acts: bfloat16 [65536, 4096], P('dp', 'fisher'), may hold values from -6 to 6
- cotangent: bfloat16 [65536, 4096], P('dp'), may hold values from -6 to 6
- out_weight: bfloat16 [4096, 4096], P('fisher', 'dp'), may hold values from -0.09375 to 0.09375
- proj_in: bfloat16 [4096, 64], P('fisher'), may hold values from -0.09375 to 0.09375
- proj_out: bfloat16 [4096, 64], replicated, may hold values from -0.09375 to 0.09375
- panels: bfloat16 [4096, 4096], P('dp', 'fisher'), may hold values from -0.09375 to 0.09375
Outputs:
- act_grad: bfloat16 [65536, 4096], P('dp', 'fisher')
- fisher_tile: float32 [4096, 4096], P('dp', 'fisher')
- scores: float32 [128, 4096], P('dp', 'fisher')
All inputs are finite; a program needn't handle non-finite values.
Results may differ from a plain program's by a relative error of at most 0.0048.
Values may be sent and summed in bfloat16 or wider, within the bound.
A program may use at most 128 MiB of HBM per device.

v0:
```python
import math

import jax
import jax.numpy as jnp
from jax import lax
from jax.sharding import PartitionSpec as P

LEN = 512


def contract_rows(left, right):
    return lax.dot_general(
        left, right, (((0,), (0,)), ((), ())), preferred_element_type=jnp.float32
    )


def per_device(acts, cotangent, out_weight, proj_in, proj_out, panels):
    tok_rows = acts.shape[0]
    width_in = proj_in.shape[1]
    width_out = proj_out.shape[1]
    width_all = width_in * width_out
    ex_local = tok_rows // LEN
    dp_count = lax.axis_size("dp")
    fisher_count = lax.axis_size("fisher")
    fisher_place = lax.axis_index("fisher")
    examples_all = ex_local * dp_count
    act_grad = lax.dot_general(
        cotangent,
        lax.all_gather(out_weight, "dp", axis=1, tiled=True),
        (((1,), (1,)), ((), ())),
        preferred_element_type=jnp.float32,
    ).astype(jnp.bfloat16)
    in_part = jnp.dot(acts, proj_in, preferred_element_type=jnp.float32)
    out_proj = jnp.dot(cotangent, proj_out, preferred_element_type=jnp.float32)
    out_each = out_proj.reshape(ex_local, LEN, width_out)
    scale = 1.0 / math.sqrt(LEN)
    in_proj = lax.psum(in_part, "fisher")
    in_each = in_proj.reshape(ex_local, LEN, width_in)
    summed = jnp.einsum("eta,etb->eab", out_each, in_each, precision=lax.Precision.HIGHEST)
    grads = (summed * scale).reshape(ex_local, width_all).astype(jnp.bfloat16)
    tile_cols = width_all // fisher_count
    col_block = lax.dynamic_slice_in_dim(grads, fisher_place * tile_cols, tile_cols, 1)
    gram = lax.psum_scatter(contract_rows(grads, col_block), "dp", scatter_dimension=0, tiled=True)
    fisher_tile = gram * (1.0 / examples_all)
    scores = jnp.dot(
        grads, lax.all_gather(panels, "dp", axis=0, tiled=True), preferred_element_type=jnp.float32
    )
    return (act_grad, fisher_tile, scores)


def solution(mesh):
    return jax.shard_map(
        per_device,
        mesh=mesh,
        in_specs=(
            P("dp", "fisher"),
            P("dp", None),
            P("fisher", "dp"),
            P("fisher", None),
            P(),
            P("dp", "fisher"),
        ),
        out_specs=(P("dp", "fisher"), P("dp", "fisher"), P("dp", "fisher")),
        check_vma=False,
    )
```

profile of v0, /device:TPU:1, one launch (start us, length us, event | category | flops | bytes accessed | tf_op | source)
XLA Modules:
  0.0 275.9 jit_solution(7136812686052108198)
XLA Ops:
  8.0 0.0 copy-start
  8.0 0.0 copy-start.1
  8.0 0.0 all-reduce.2.cloned.1.call-start
  8.1 1.5 copy-done
  9.6 1.6 fusion.7
  11.2 0.8 copy.18
  12.0 0.0 all-reduce.2.cloned.1.call-update
  12.0 0.0 all-gather.5.cloned.1.call-start
  12.1 0.5 all-gather.5.cloned.1.call-update
  12.6 0.0 all-gather.3.cloned.1.call-start
  12.7 0.5 all-gather.3.cloned.1.call-update
  13.2 0.0 reduce-scatter.2.cloned.1.call-start
  13.3 0.0 copy-done.1
  13.3 10.9 %fusion.6 = f32[2048,64]{0,1:T(8,128)S(1)} fusion(bf16[2048,4096]{1,0:T(8,128)(2,1)} %param.7, bf16[4096,64]{0,1:T(8,128)(2,1)S(1)} %copy-done.1), kind=kOutput, calls=%fused_computation.10 | convolution fusion | flops 1073741824 | bytes 17825792 | tf_op jit(solution)/shard_map/dot_general | solution.py:34
  24.2 69.8 %all-reduce.2.cloned.1.call-done = f32[4,512,64]{1,2,0:T(8,128)} async-done(((f32[4,512,64]{1,2,0:T(8,128)}), f32[4,512,64]{1,2,0:T(8,128)}) %all-reduce.2.cloned.1.call-update) | async-done | bytes 524304 | tf_op jit(solution)/shard_map/psum | solution.py:37
  94.1 1.7 fusion
  95.7 0.1 convert_element_type.11
  95.8 4.5 %fusion.3 = f32[4096,512]{1,0:T(8,128)} fusion(bf16[4,4096]{1,0:T(4,128)(2,1)S(1)} %convert_element_type.11, s32[]{:T(128)S(6)} %select_n.3), kind=kOutput, calls=%fused_computation.7 | convolution fusion | flops 16777216 | bytes 8425476 | tf_op jit(solution)/shard_map/dot_general | solution.py:12
  100.4 0.0 reduce-scatter.2.cloned.1.call-update
  100.4 0.0 all-gather.5.cloned.1.call-done
  100.4 3.4 %fusion.8 = f32[4,512]{1,0:T(4,128)} fusion(bf16[4,4096]{1,0:T(4,128)(2,1)S(1)} %convert_element_type.11, bf16[4096,512]{1,0:T(8,128)(2,1)} %all-gather.5.cloned.1.call-done), kind=kOutput, calls=%fused_computation.12 | convolution fusion | flops 16777216 | bytes 4235264 | tf_op jit(solution)/shard_map/dot_general | solution.py:45
  103.9 41.0 %all-gather.3.cloned.1.call-done = bf16[512,4096]{1,0:T(8,128)(2,1)} async-done(((bf16[512,128]{1,0:T(8,128)(2,1)}), bf16[512,4096]{1,0:T(8,128)(2,1)}) %all-gather.3.cloned.1.call-update) | async-done | bytes 4194320 | tf_op jit(solution)/shard_map/all_gather | solution.py:29
  144.8 14.6 %convolution_convert_fusion = bf16[2048,512]{1,0:T(8,128)(2,1)} fusion(bf16[2048,4096]{1,0:T(8,128)(2,1)} %param.7, bf16[512,4096]{1,0:T(8,128)(2,1)} %all-gather.3.cloned.1.call-done), kind=kOutput, calls=%fused_computation | convolution fusion | flops 8590983168 | bytes 23068672 | tf_op jit(solution)/shard_map/dot_general | solution.py:27
  159.4 107.3 %reduce-scatter.2.cloned.1.call-done = f32[128,512]{1,0:T(8,128)} async-done(((f32[4096,512]{1,0:T(8,128)}), f32[128,512]{1,0:T(8,128)}) %reduce-scatter.2.cloned.1.call-update) | async-done | bytes 262160 | tf_op jit(solution)/shard_map/reduce_scatter | solution.py:43
  266.7 1.7 broadcast_multiply_fusion
Async XLA Ops:
  8.0 1.6 copy-start
  8.0 5.3 %copy-start.1 = (bf16[4096,64]{0,1:T(8,128)(2,1)S(1)}, bf16[4096,64]{0,1:T(8,128)(2,1)}, u32[]{:S(2)}) copy-start(bf16[4096,64]{0,1:T(8,128)(2,1)} %param.10) | copy-start | bytes 1572868
  8.0 86.0 %all-reduce.2.cloned.1.call-start = ((), (), s32[]{:S(2)}) async-start(), calls=%async_computation.2 | async-start | bytes 1048576 | tf_op jit(solution)/shard_map/psum | solution.py:37
  12.0 88.4 %all-gather.5.cloned.1.call-start = ((), (), s32[]{:S(2)}) async-start(), calls=%async_computation.4 | async-start | bytes 4325376 | tf_op jit(solution)/shard_map/all_gather | solution.py:46
  12.6 132.2 %all-gather.3.cloned.1.call-start = ((), (), s32[]{:S(2)}) async-start(), calls=%async_computation.1 | async-start | bytes 4325376 | tf_op jit(solution)/shard_map/all_gather | solution.py:29
  13.2 253.5 %reduce-scatter.2.cloned.1.call-start = ((), (), s32[]{:S(2)}) async-start(), calls=%async_computation.3 | async-start | bytes 8650752 | tf_op jit(solution)/shard_map/reduce_scatter | solution.py:43
Sparse Core Ops, SparseCore 0:
  12.2 81.8 all-reduce.1
Sparse Core Ops, SparseCore 1:
  15.1 65.1 all-gather.4
  82.6 62.2 all-gather.2
  149.2 117.4 reduce-scatter.1
where the time goes:
time: 276 us
  waiting for transfers between devices  219 us (79%)
  matrix products  36.8 us (13%)
  between operations  15.7 us (6%)
    reduce_scatter x1, waiting for transfers between devices, per_device(): lax.psum_scatter(contract_rows(grads, col_block), 'dp', scatter_dimension...  107 us
    psum x1, waiting for transfers between devices, per_device(): in_proj = lax.psum(in_part, 'fisher')  69.8 us
    all_gather x1, waiting for transfers between devices, per_device(): lax.all_gather(out_weight, 'dp', axis=1, tiled=True)  41 us
    dot_general x1, matrix products, per_device(): lax.dot_general(cotangent, lax.all_gather(out_weight, 'dp', axis=1, tiled...  14.6 us
    dot_general x1, matrix products, per_device(): out_proj = jnp.dot(cotangent, proj_out, preferred_element_type=jnp.float32)  10.9 us
  transfers between devices with their start and end apart: 4, of which 3 were waited for; matrix products, arithmetic and copies ran while one was open for 13% of the time, Pallas kernels for 0%

commit v1 on v0

v1 whole, which is shorter than its diff:
```python
import math

import jax
import jax.numpy as jnp
from jax import lax
from jax.sharding import PartitionSpec as P

LEN = 512


def contract_rows(left, right):
    return lax.dot_general(
        left, right, (((0,), (0,)), ((), ())), preferred_element_type=jnp.float32
    )


def per_device(acts, cotangent, out_weight, proj_in, proj_out, panels):
    tok_rows = acts.shape[0]
    width_in = proj_in.shape[1]
    width_out = proj_out.shape[1]
    width_all = width_in * width_out
    ex_local = tok_rows // LEN
    dp_count = lax.axis_size("dp")
    fisher_count = lax.axis_size("fisher")
    dp_place = lax.axis_index("dp")
    fisher_place = lax.axis_index("fisher")
    examples_all = ex_local * dp_count
    in_part = jnp.dot(acts, proj_in, preferred_element_type=jnp.float32)
    out_proj = jnp.dot(cotangent, proj_out, preferred_element_type=jnp.float32)
    out_each = out_proj.reshape(ex_local, LEN, width_out)
    in_each = in_part.reshape(ex_local, LEN, width_in)
    part = jnp.einsum("eta,etb->eab", out_each, in_each, precision=lax.Precision.HIGHEST)
    summed = lax.psum(part, "fisher")
    grads = (summed * (1.0 / math.sqrt(LEN))).reshape(ex_local, width_all).astype(jnp.bfloat16)
    everyone = lax.all_gather(grads, "dp", axis=0, tiled=True)
    tile_cols = width_all // fisher_count
    tile_rows = width_all // dp_count
    col_block = lax.dynamic_slice_in_dim(everyone, fisher_place * tile_cols, tile_cols, 1)
    row_block = lax.dynamic_slice_in_dim(everyone, dp_place * tile_rows, tile_rows, 1)
    fisher_tile = contract_rows(row_block, col_block) * (1.0 / examples_all)
    score_part = jnp.dot(row_block, panels, preferred_element_type=jnp.float32)
    scores = lax.psum_scatter(score_part, "dp", scatter_dimension=0, tiled=True)
    act_grad = lax.dot_general(
        cotangent,
        lax.all_gather(out_weight, "dp", axis=1, tiled=True),
        (((1,), (1,)), ((), ())),
        preferred_element_type=jnp.float32,
    ).astype(jnp.bfloat16)
    return (act_grad, fisher_tile, scores)


def solution(mesh):
    return jax.shard_map(
        per_device,
        mesh=mesh,
        in_specs=(
            P("dp", "fisher"),
            P("dp", None),
            P("fisher", "dp"),
            P("fisher", None),
            P(),
            P("dp", "fisher"),
        ),
        out_specs=(P("dp", "fisher"), P("dp", "fisher"), P("dp", "fisher")),
        check_vma=False,
    )
```

time: 276 us -> 530 us (1.92)
  waiting for transfers between devices: 219 us -> 479 us
  matrix products: 36.8 us -> 30.3 us
    unnamed x4 -> x5, waiting for transfers between devices: 1.09 us -> 277 us
    reduce_scatter x1 -> x0, waiting for transfers between devices: 107 us -> none  [per_device(): lax.psum_scatter(contract_rows(grads, col_block), 'dp', scatter_dimension...]
    all_gather x1, waiting for transfers between devices: 0.03 us -> 58.5 us  [per_device(): everyone = lax.all_gather(grads, 'dp', axis=0, tiled=True)]
    all_gather x1, waiting for transfers between devices: 41 us -> 65.2 us  [per_device(): lax.all_gather(out_weight, 'dp', axis=1, tiled=True)]
    psum x1, waiting for transfers between devices: 69.8 us -> 77.6 us  [per_device(): summed = lax.psum(part, 'fisher')]
  transfers between devices with their start and end apart: 4 -> 4, of which waited for: 3 -> 4; matrix products, arithmetic and copies ran while one was open for 13% -> 1% of each run, Pallas kernels for 0% -> 0%
where the time goes in v1:
time: 530 us
  waiting for transfers between devices  479 us (90%)
  matrix products  30.3 us (6%)
  between operations  14.5 us (3%)
  local copies, waits for them, and re-layouts  5.52 us (1%)
    unnamed x5, waiting for transfers between devices  277 us
    psum x1, waiting for transfers between devices, per_device(): summed = lax.psum(part, 'fisher')  77.6 us
    all_gather x1, waiting for transfers between devices, per_device(): lax.all_gather(out_weight, 'dp', axis=1, tiled=True)  65.2 us
    all_gather x1, waiting for transfers between devices, per_device(): everyone = lax.all_gather(grads, 'dp', axis=0, tiled=True)  58.5 us
    dot_general x1, matrix products, per_device(): lax.dot_general(cotangent, lax.all_gather(out_weight, 'dp', axis=1, tiled...  14.6 us
    dot_general x1, matrix products, per_device(): out_proj = jnp.dot(cotangent, proj_out, preferred_element_type=jnp.float32)  11 us
  transfers between devices with their start and end apart: 4, of which 4 were waited for; matrix products, arithmetic and copies ran while one was open for 1% of the time, Pallas kernels for 0%

profile of v1, /device:TPU:1, one launch (start us, length us, event | category | flops | bytes accessed | tf_op | source)
XLA Modules:
  0.0 530.1 jit_solution(1092583051744811826)
XLA Ops:
  7.2 0.0 copy-start
  7.2 0.0 all-reduce.4.cloned.1.call-start
  7.2 1.5 copy-done
  8.8 1.6 fusion.12
  10.3 0.0 copy-start.1
  10.4 11.0 %fusion.11 = f32[2048,64]{0,1:T(8,128)S(1)} fusion(bf16[2048,4096]{1,0:T(8,128)(2,1)} %param.7, bf16[4096,64]{0,1:T(8,128)(2,1)} %param.10), kind=kOutput, calls=%fused_computation.15 | convolution fusion | flops 1073741824 | bytes 17825792 | tf_op jit(solution)/shard_map/dot_general | solution.py:29
  21.4 0.0 copy-start.2
  21.4 1.3 fusion
  22.7 0.0 all-reduce.4.cloned.1.call-update
  22.7 0.0 all-gather.6.cloned.1.call-start
  22.8 77.6 %all-reduce.4.cloned.1.call-done = f32[4,64,64]{2,1,0:T(8,128)} async-done(((f32[4,64,64]{2,1,0:T(8,128)}), f32[4,64,64]{2,1,0:T(8,128)}) %all-reduce.4.cloned.1.call-update) | async-done | bytes 65552 | tf_op jit(solution)/shard_map/psum | solution.py:33
  100.3 0.9 multiply_convert_fusion
  101.2 0.7 reshape.16
  102.0 0.0 all-gather.6.cloned.1.call-update
  102.0 0.0 all-reduce.6.cloned.1.call-start
  102.0 58.5 %all-gather.6.cloned.1.call-done = bf16[32,4,4096]{2,1,0:T(4,128)(2,1)} async-done(((bf16[1,4,4096]{2,1,0:T(4,128)(2,1)}), bf16[32,4,4096]{2,1,0:T(4,128)(2,1)}) %all-gather.6.cloned.1.call-update) | async-done | bytes 1048592 | tf_op jit(solution)/shard_map/all_gather | solution.py:35
  160.6 1.3 reshape.17
  161.9 0.0 copy-done.1
  161.9 0.9 fusion.6
  162.8 0.0 all-reduce.6.cloned.1.call-update
  162.9 0.0 all-gather.4.cloned.1.call-start
  162.9 0.5 all-gather.4.cloned.1.call-update
  163.4 0.0 copy-done.2
  163.5 0.6 dynamic-slice
  164.7 0.9 convolution_multiply_fusion
  165.6 276.8 %all-reduce.6.cloned.1.call-done = f32[128,512]{1,0:T(8,128)} async-done(((f32[128,512]{1,0:T(8,128)}), f32[128,512]{1,0:T(8,128)}) %all-reduce.6.cloned.1.call-update) | async-done | bytes 262160
  442.5 1.3 constant_dynamic-slice_fusion
  443.8 65.2 %all-gather.4.cloned.1.call-done = bf16[512,4096]{1,0:T(8,128)(2,1)} async-done(((bf16[512,128]{1,0:T(8,128)(2,1)}), bf16[512,4096]{1,0:T(8,128)(2,1)}) %all-gather.4.cloned.1.call-update) | async-done | bytes 4194320 | tf_op jit(solution)/shard_map/all_gather | solution.py:45
  509.0 14.6 %convolution_convert_fusion = bf16[2048,512]{1,0:T(8,128)(2,1)} fusion(bf16[2048,4096]{1,0:T(8,128)(2,1)} %param.7, bf16[512,4096]{1,0:T(8,128)(2,1)} %all-gather.4.cloned.1.call-done), kind=kOutput, calls=%fused_computation | convolution fusion | flops 8590983168 | bytes 23068672 | tf_op jit(solution)/shard_map/dot_general | solution.py:43
Async XLA Ops:
  7.2 1.6 copy-start
  7.2 93.1 %all-reduce.4.cloned.1.call-start = ((), (), s32[]{:S(2)}) async-start(), calls=%async_computation.1 | async-start | bytes 262144 | tf_op jit(solution)/shard_map/psum | solution.py:33
  10.3 151.6 %copy-start.1 = (bf16[128,512]{1,0:T(8,128)(2,1)S(1)}, bf16[128,512]{1,0:T(8,128)(2,1)}, u32[]{:S(2)}) copy-start(bf16[128,512]{1,0:T(8,128)(2,1)} %param.11) | copy-start | bytes 393220
  21.4 142.1 %copy-start.2 = (u32[256]{0:T(256)S(1)}, u32[256]{0:T(256)}, u32[]{:S(2)}) copy-start(u32[256]{0:T(256)} %constant.23) | copy-start | bytes 3076
  22.7 137.9 %all-gather.6.cloned.1.call-start = ((), (), s32[]{:S(2)}) async-start(), calls=%async_computation.2 | async-start | bytes 1081344 | tf_op jit(solution)/shard_map/all_gather | solution.py:35
  102.0 340.5 %all-reduce.6.cloned.1.call-start = ((), (), s32[]{:S(2)}) async-start(), calls=%async_computation.3 | async-start | bytes 524288
  162.9 346.2 %all-gather.4.cloned.1.call-start = ((), (), s32[]{:S(2)}) async-start(), calls=%async_computation | async-start | bytes 4325376 | tf_op jit(solution)/shard_map/all_gather | solution.py:45
Sparse Core Ops, SparseCore 0:
  22.8 77.4 all-reduce.3
  103.8 56.7 all-gather.5
  164.0 278.4 all-reduce.5
  444.8 64.1 all-gather.3

commit v2 on v0

v2 whole, which is shorter than its diff:
```python
import functools
import math

import jax
import jax.numpy as jnp
from jax import lax
from jax.experimental import pallas as pl
from jax.experimental.pallas import tpu as pltpu
from jax.sharding import PartitionSpec as P

LEN = 512
MESH = pl.DeviceIdType.MESH
F32 = jnp.float32
BF16 = jnp.bfloat16
ROWS = 512


def dot(a, b, ca=1, cb=0, precision=None):
    return lax.dot_general(
        a, b, (((ca,), (cb,)), ((), ())), preferred_element_type=F32, precision=precision
    )


def kernel(
    acts_h, cot_h, w_h, pin_h, pout_h, pan_h,
    act_o, fish_o, score_o,
    acts, cot, w_own, pin, pout, pan,
    wg, acc, act_v,
    q_part, send1, recv1, g_own, g_row, send2, g_all, s_part, s_pair, s_sum, recv3, fin,
    in_sem, cot_sem, out_sem,
    w_send, rz, rx, rsib,
    e_send, e_recv,
):
    i = lax.axis_index("dp")
    j = lax.axis_index("fisher")
    c = lax.rem(i, 2)
    q = i // 2
    zh = lax.rem(q, 4)
    x = q // 4
    sib = (i + 1 - 2 * c, j)

    def chip(dx, dz):
        return lax.rem(x + dx + 4, 4) * 4 + lax.rem(zh + dz + 4, 4)

    def dev(dx, dz):
        return (chip(dx, dz) * 2 + c, j)

    loads = [
        pltpu.make_async_copy(w_h, w_own, in_sem.at[0]),
        pltpu.make_async_copy(pout_h, pout, in_sem.at[1]),
        pltpu.make_async_copy(pin_h, pin, in_sem.at[2]),
        pltpu.make_async_copy(acts_h, acts, in_sem.at[3]),
        pltpu.make_async_copy(pan_h, pan, in_sem.at[4]),
    ]
    for load in loads[:4]:
        load.start()

    def cot_load(e):
        rows = pl.ds(e * LEN, LEN)
        return pltpu.make_async_copy(cot_h.at[rows], cot.at[rows], cot_sem.at[e])

    for e in range(4):
        cot_load(e).start()
    loads[4].start()

    barrier = pltpu.get_barrier_semaphore()
    pl.semaphore_signal(barrier, inc=1, device_id=sib, device_id_type=MESH)

    @pl.loop(1, 8)
    def _(s):
        pl.semaphore_signal(barrier, inc=1, device_id=(i, lax.rem(j + s, 8)), device_id_type=MESH)

    @pl.loop(1, 16)
    def _(s):
        pl.semaphore_signal(
            barrier, inc=1, device_id=(lax.rem(q + s, 16) * 2 + c, j), device_id_type=MESH
        )

    eye = jnp.where(
        lax.broadcasted_iota(jnp.int32, (128, 128), 0) == lax.broadcasted_iota(jnp.int32, (128, 128), 1),
        1.0, 0.0,
    ).astype(BF16)
    loads[0].wait()

    def wrows(chip_index, core, half=None):
        start = chip_index * 256 + core * 128
        if half is None:
            return wg.at[pl.ds(pl.multiple_of(start, 128), 128)]
        return wg.at[pl.ds(pl.multiple_of(start + 64 * half, 64), 64)]

    wg[pl.ds(pl.multiple_of(q * 256 + c * 128, 128), 128), :] = dot(eye, w_own[...], 1, 1).astype(BF16)
    pl.semaphore_wait(barrier, 23)

    sent = []

    def push(ref, to, recv):
        copy = pltpu.make_async_remote_copy(
            src_ref=ref, dst_ref=ref, send_sem=w_send.at[len(sent)], recv_sem=recv,
            device_id=to, device_id_type=MESH,
        )
        copy.start()
        sent.append(copy)

    def arrive(ref, sem):
        pltpu.make_async_copy(ref, ref, sem).wait()

    DZ = (0, -1, 1, 2)
    DX = (0, -1, 1, 2)

    def to_x(m):
        push(wrows(chip(0, DZ[m]), c), dev(1, 0), rx.at[m, 0])
        push(wrows(chip(0, DZ[m]), c), dev(-1, 0), rx.at[m, 1])

    def to_sib(m, k):
        push(wrows(chip(DX[k], DZ[m]), c), sib, rsib.at[m, k])

    push(wrows(q, c), dev(0, 1), rz.at[0])
    push(wrows(q, c), dev(0, -1), rz.at[1])
    to_x(0)
    to_sib(0, 0)

    def x_near(m):
        arrive(wrows(chip(-1, DZ[m]), c), rx.at[m, 0])
        push(wrows(chip(-1, DZ[m]), c, 0), dev(1, 0), rx.at[m, 2])
        to_sib(m, 1)
        arrive(wrows(chip(1, DZ[m]), c), rx.at[m, 1])
        push(wrows(chip(1, DZ[m]), c, 1), dev(-1, 0), rx.at[m, 3])
        to_sib(m, 2)

    def x_far(m):
        arrive(wrows(chip(2, DZ[m]), c, 0), rx.at[m, 2])
        arrive(wrows(chip(2, DZ[m]), c, 1), rx.at[m, 3])
        to_sib(m, 3)

    def z_near():
        arrive(wrows(chip(0, -1), c), rz.at[0])
        push(wrows(chip(0, -1), c, 0), dev(0, 1), rz.at[2])
        to_x(1)
        arrive(wrows(chip(0, 1), c), rz.at[1])
        push(wrows(chip(0, 1), c, 1), dev(0, -1), rz.at[3])
        to_x(2)
        to_sib(1, 0)
        to_sib(2, 0)

    def z_far():
        arrive(wrows(chip(0, 2), c, 0), rz.at[2])
        arrive(wrows(chip(0, 2), c, 1), rz.at[3])
        to_x(3)
        to_sib(3, 0)

    loads[1].wait()
    row = lax.broadcasted_iota(jnp.int32, (64, 64), 0)
    col = lax.broadcasted_iota(jnp.int32, (64, 64), 1)
    even_odd = jnp.where(col == lax.rem(row, 32) * 2 + row // 32, 1.0, 0.0).astype(BF16)
    pout[...] = dot(even_odd, pout[...]).astype(BF16)
    loads[2].wait()
    loads[3].wait()

    def example(e, _):
        cot_load(e).wait()
        rows = pl.ds(pl.multiple_of(e * LEN, LEN), LEN)
        op = dot(cot[rows, :], pout[...], 1, 1)
        ip = dot(acts[rows, :], pin[...], 1, 1)
        part = dot(op, ip, 0, 0, lax.Precision.HIGHEST)
        q_part[e] = jnp.concatenate([part[:32], part[32:]], axis=1)
        return 0

    lax.fori_loop(0, 2, example, 0)
    x_near(0)
    lax.fori_loop(2, 4, example, 0)
    z_near()
    for jj in range(8):
        for e in range(4):
            send1[jj, e * 4:e * 4 + 4, :] = q_part[e, jj * 4:jj * 4 + 4, :]

    def exchange(n, copy_of, stage):
        def go(s, _):
            copy_of(s).start()
            return 0
        lax.fori_loop(1, n, go, 0)

    def done_sending(n, copy_of):
        def go(s, _):
            copy_of(s).wait_send()
            return 0
        lax.fori_loop(1, n, go, 0)

    def remote(src, dst, to, stage, s):
        return pltpu.make_async_remote_copy(
            src_ref=src, dst_ref=dst, send_sem=e_send.at[stage, s], recv_sem=e_recv.at[stage],
            device_id=to, device_id_type=MESH,
        )

    def copy1(s):
        to = lax.rem(j + s, 8)
        return remote(send1.at[to], recv1.at[j], (i, to), 0, s)

    def copy1b(s):
        return remote(g_own, g_row.at[j], (i, lax.rem(j + s, 8)), 1, s)

    def copy2(s):
        to = lax.rem(q + s, 16)
        return remote(send2.at[to], g_all.at[c, q], (to * 2 + c, j), 2, s)

    def copy2c():
        return remote(g_all.at[c], g_all.at[c], sib, 3, 0)

    def copy3c():
        return remote(s_part.at[1 - c], s_pair, sib, 4, 0)

    def copy3(s):
        to = lax.rem(q + s, 16)
        rows = pl.ds(pl.multiple_of(to * 8, 8), 8)
        return remote(s_sum.at[rows], recv3.at[q], (to * 2 + c, j), 5, s)

    def copy3f():
        return remote(fin.at[c], fin.at[c], sib, 6, 0)

    def blocks(m, k):
        if (m, k) != (0, 0):
            pass
        arrive(wrows(chip(DX[k], DZ[m]), 1 - c), rsib.at[m, k])

    def a_pass(first, second, mode):
        blocks(*first)
        blocks(*second)
        ka = pl.ds(pl.multiple_of(chip(DX[first[1]], DZ[first[0]]) * 256, 256), 256)
        kb = pl.ds(pl.multiple_of(chip(DX[second[1]], DZ[second[0]]) * 256, 256), 256)

        def step(t, _):
            rows = pl.ds(pl.multiple_of(t * ROWS, ROWS), ROWS)
            new = dot(cot[rows, ka], wg[ka, :]) + dot(cot[rows, kb], wg[kb, :])
            if mode == 0:
                acc[rows, :] = new
            elif mode == 1:
                acc[rows, :] += new
            else:
                act_v[rows, :] = (acc[rows, :] + new).astype(BF16)
                pltpu.make_async_copy(act_v.at[rows], act_o.at[rows], out_sem.at[t]).start()
            return 0

        lax.fori_loop(0, acc.shape[0] // ROWS, step, 0)

    exchange(8, copy1, 0)
    recv1[j] = send1[j]
    x_far(0)
    a_pass((0, 0), (0, 1), 0)

    arrive(recv1.at[pl.ds(0, 7)], e_recv.at[0])
    total = recv1[0]
    for s in range(1, 8):
        total = total + recv1[s]
    mine = (total * (1.0 / math.sqrt(LEN))).astype(BF16)
    g_own[...] = mine
    exchange(8, copy1b, 1)
    g_row[j] = mine
    z_far()
    a_pass((0, 2), (1, 0), 1)
    x_near(1)

    arrive(g_row.at[pl.ds(0, 7)], e_recv.at[1])
    for to in range(16):
        send2[to, 0] = g_row[to // 2]
        send2[to, 1] = mine
    exchange(16, copy2, 2)
    g_all[c, q] = send2[q]
    x_near(2)
    a_pass((2, 0), (0, 3), 1)

    arrive(g_all.at[c, pl.ds(0, 15)], e_recv.at[2])
    copy2c().start()
    x_far(1)
    a_pass((3, 0), (1, 1), 1)
    x_far(2)

    arrive(g_all.at[1 - c], e_recv.at[3])
    m = lax.broadcasted_iota(jnp.int32, (128, 512), 0)
    n = lax.broadcasted_iota(jnp.int32, (128, 512), 1)
    base = lax.rem(m // 4, 2) * 256 + (m // 8) * 16 + lax.rem(m, 4) * 4

    def select(r):
        return jnp.where(n == base + r, 1.0, 0.0).astype(BF16)

    row_tiles = g_all[:, :, 0].reshape(512, 128)
    col_tiles = g_all[:, :, 1].reshape(512, 128)
    g_rows = dot(select(lax.rem(i, 4)), row_tiles).astype(BF16)
    loads[4].wait()
    s_part[0] = dot(g_rows, pan[:, :256])
    s_part[1] = dot(g_rows, pan[:, 256:])
    copy3c().start()
    for r in range(4):
        g_cols = dot(select(r), col_tiles).astype(BF16)
        fish_o[:, r * 128:(r + 1) * 128] = dot(g_rows, g_cols, 0, 0) * (1.0 / 128)
    x_near(3)
    a_pass((1, 2), (2, 1), 1)

    arrive(s_pair, e_recv.at[4])
    s_sum[...] = s_part[c] + s_pair[...]
    exchange(16, copy3, 5)
    recv3[q] = s_sum[pl.ds(pl.multiple_of(q * 8, 8), 8), :]
    x_far(3)
    a_pass((2, 2), (1, 3), 1)

    arrive(recv3.at[pl.ds(0, 15)], e_recv.at[5])
    total = recv3[0]
    for s in range(1, 16):
        total = total + recv3[s]
    fin[c] = total
    copy3f().start()
    a_pass((2, 3), (3, 1), 1)

    arrive(fin.at[1 - c], e_recv.at[6])
    for h in range(2):
        score_o[:, h * 256:(h + 1) * 256] = jnp.where(c == 0, fin[h, :4], fin[h, 4:])
    a_pass((3, 2), (3, 3), 2)

    for copy in sent:
        copy.wait_send()
    done_sending(8, copy1)
    done_sending(8, copy1b)
    done_sending(16, copy2)
    copy2c().wait_send()
    copy3c().wait_send()
    done_sending(16, copy3)
    copy3f().wait_send()

    def wrote(t, _):
        rows = pl.ds(pl.multiple_of(t * ROWS, ROWS), ROWS)
        pltpu.make_async_copy(act_v.at[rows], act_o.at[rows], out_sem.at[t]).wait()
        return 0

    lax.fori_loop(0, acc.shape[0] // ROWS, wrote, 0)


def per_device(acts, cotangent, out_weight, proj_in, proj_out, panels):
    rows, wide = cotangent.shape
    feats = acts.shape[1]
    any_spec = pl.BlockSpec(memory_space=pl.ANY)
    vmem_spec = pl.BlockSpec(memory_space=pltpu.VMEM)
    dma = pltpu.SemaphoreType.DMA
    return pl.pallas_call(
        kernel,
        out_shape=(
            jax.ShapeDtypeStruct((rows, feats), BF16),
            jax.ShapeDtypeStruct((128, 512), F32),
            jax.ShapeDtypeStruct((4, 512), F32),
        ),
        in_specs=[any_spec] * 6,
        out_specs=(any_spec, vmem_spec, vmem_spec),
        scratch_shapes=[
            pltpu.VMEM((rows, feats), BF16),
            pltpu.VMEM((rows, wide), BF16),
            pltpu.VMEM((feats, 128), BF16),
            pltpu.VMEM((64, feats), BF16),
            pltpu.VMEM((64, wide), BF16),
            pltpu.VMEM((128, 512), BF16),
            pltpu.VMEM((wide, feats), BF16),
            pltpu.VMEM((rows, feats), F32),
            pltpu.VMEM((rows, feats), BF16),
            pltpu.VMEM((4, 32, 128), F32),
            pltpu.VMEM((8, 16, 128), F32),
            pltpu.VMEM((8, 16, 128), F32),
            pltpu.VMEM((16, 128), BF16),
            pltpu.VMEM((8, 16, 128), BF16),
            pltpu.VMEM((16, 2, 16, 128), BF16),
            pltpu.VMEM((2, 16, 2, 16, 128), BF16),
            pltpu.VMEM((2, 128, 256), F32),
            pltpu.VMEM((128, 256), F32),
            pltpu.VMEM((128, 256), F32),
            pltpu.VMEM((16, 8, 256), F32),
            pltpu.VMEM((2, 8, 256), F32),
            dma((5,)),
            dma((4,)),
            dma((rows // ROWS,)),
            dma((36,)),
            dma((4,)),
            dma((4, 4)),
            dma((4, 4)),
            dma((7, 16)),
            dma((7,)),
        ],
        compiler_params=pltpu.CompilerParams(
            collective_id=0, has_side_effects=True, vmem_limit_bytes=60 * 1024 * 1024
        ),
        cost_estimate=pl.CostEstimate(
            flops=2 * rows * wide * (feats + 64), bytes_accessed=26 * 2**20, transcendentals=0
        ),
    )(acts, cotangent, out_weight, proj_in.T, proj_out.T, panels)


def solution(mesh):
    return jax.shard_map(
        per_device,
        mesh=mesh,
        in_specs=(
            P("dp", "fisher"),
            P("dp", None),
            P("fisher", "dp"),
            P("fisher", None),
            P(),
            P("dp", "fisher"),
        ),
        out_specs=(P("dp", "fisher"), P("dp", "fisher"), P("dp", "fisher")),
        check_vma=False,
    )
```

time: 276 us -> 59 us (0.21)
  waiting for transfers between devices: 219 us -> 0 us
  Pallas kernels: 0 us -> 53.8 us
  matrix products: 36.8 us -> 0 us
  between operations: 15.7 us -> 0.66 us
    reduce_scatter x1 -> x0, waiting for transfers between devices: 107 us -> none  [per_device(): lax.psum_scatter(contract_rows(grads, col_block), 'dp', scatter_dimension...]
    psum x1 -> x0, waiting for transfers between devices: 69.8 us -> none  [per_device(): in_proj = lax.psum(in_part, 'fisher')]
    pallas_call x0 -> x1, Pallas kernels: none -> 53.8 us  [per_device(): pl.pallas_call(kernel, out_shape=(jax.ShapeDtypeStruct((rows, feats), BF1...]
    all_gather x2 -> x0, waiting for transfers between devices: 41 us -> none  [the longest x1 41 us: per_device(): lax.all_gather(out_weight, 'dp', axis=1, tiled=True)]
    dot_general x6 -> x0, matrix products: 36.8 us -> none  [the longest x1 14.6 us: per_device(): lax.dot_general(cotangent, lax.all_gather(out_weight, 'dp', axis=1, tiled...]
    unnamed x4 -> x7, local copies, waits for them, and re-layouts: 1.54 us -> 4.39 us
  transfers between devices with their start and end apart: 4 -> 0, of which waited for: 3 -> 0; matrix products, arithmetic and copies ran while one was open for 13% -> 0% of each run, Pallas kernels for 0% -> 0%
where the time goes in v2:
time: 59 us; the launch traced here: 58.9 us
  Pallas kernels  53.8 us (91%)
  local copies, waits for them, and re-layouts  4.39 us (7%)
  between operations  0.66 us (1%)
    pallas_call x1, Pallas kernels, per_device(): pl.pallas_call(kernel, out_shape=(jax.ShapeDtypeStruct((rows, feats), BF1...  53.8 us
    unnamed x7, local copies, waits for them, and re-layouts  4.39 us

profile of v2, /device:TPU:1, one launch (start us, length us, event | category | flops | bytes accessed | tf_op | source)
XLA Modules:
  0.0 58.9 jit_solution(3249068636097035171)
XLA Ops:
  0.6 53.8 %shard_map.85 = (bf16[2048,512]{1,0:T(8,128)(2,1)}, f32[128,512]{1,0:T(8,128)}, f32[4,512]{1,0:T(4,128)}) custom-call(bf16[2048,512]{1,0:T(8,128)(2,1)} %acts_h.1, bf16[2048,4096]{1,0:T(8,128)(2,1)} %cot_h.1, bf16[512,128]{1,0:T(8,128)(2,1)} %w_h.1, bf16[64,512]{1,0:T(8,128)(2,1)} %bitcast.3, bf16[64,4096]{1,0:T(8,128)(2,1)} %bitcast.2, bf16[128,512]{1,0:T(8,128)(2,1)} %pan_h.1), custom_call_target="tpu_custom_call" | custom-call | flops 9663676416 | bytes 27262976 | tf_op jit(solution)/shard_map/pallas_call | solution.py:341
  54.5 0.0 copy-start
  54.5 0.0 copy-start.1
  54.5 3.1 %copy.12 = bf16[2048,512]{1,0:T(8,128)(2,1)} copy(bf16[2048,512]{1,0:T(8,128)(2,1)} %get-tuple-element.6) | data formatting | bytes 4194304
  57.6 0.0 copy-done
  57.6 0.7 %copy.13 = f32[128,512]{1,0:T(8,128)} copy(f32[128,512]{1,0:T(8,128)S(1)} %copy-done) | data formatting | bytes 524288
  58.3 0.0 copy-done.1
  58.3 0.6 %copy.14 = f32[4,512]{1,0:T(4,128)} copy(f32[4,512]{1,0:T(4,128)S(1)} %copy-done.1) | data formatting | bytes 16384
Async XLA Ops:
  54.5 3.1 %copy-start = (f32[128,512]{1,0:T(8,128)S(1)}, f32[128,512]{1,0:T(8,128)}, u32[]{:S(2)}) copy-start(f32[128,512]{1,0:T(8,128)} %get-tuple-element.7) | copy-start | bytes 786436
  54.5 3.8 %copy-start.1 = (f32[4,512]{1,0:T(4,128)S(1)}, f32[4,512]{1,0:T(4,128)}, u32[]{:S(2)}) copy-start(f32[4,512]{1,0:T(4,128)} %get-tuple-element.8) | copy-start | bytes 24580

commit v3 on v2

v3 whole, which is shorter than its diff:
```python
import functools
import math

import jax
import jax.numpy as jnp
from jax import lax
from jax.experimental import pallas as pl
from jax.experimental.pallas import tpu as pltpu
from jax.sharding import PartitionSpec as P

LEN = 512
MESH = pl.DeviceIdType.MESH
F32 = jnp.float32
BF16 = jnp.bfloat16
PIECE = 256


def dot(a, b, ca=1, cb=0, precision=None):
    return lax.dot_general(
        a, b, (((ca,), (cb,)), ((), ())), preferred_element_type=F32, precision=precision
    )


def two_parts(v):
    high = v.astype(BF16)
    return jnp.concatenate([high, (v - high.astype(F32)).astype(BF16)], axis=1)


def kernel(
    acts_h, cot_h, w_h, pin_h, pout_h, pan_h,
    act_o, fish_o, score_o,
    acts, cot, w_own, pin, pout, pan, wg, acc,
    in_send, in_recv, q_part, q_all, tiles_f, tiles, send2, g_all, s_part, s_recv,
    in_sem, cot_sem,
    w_send, rz, rx, rsib,
    e_send, e_recv,
):
    i = lax.axis_index("dp")
    j = lax.axis_index("fisher")
    c = lax.rem(i, 2)
    q = i // 2
    zh = lax.rem(q, 4)
    x = q // 4
    sib = (i + 1 - 2 * c, j)

    def chip(dx, dz):
        return lax.rem(x + dx + 4, 4) * 4 + lax.rem(zh + dz + 4, 4)

    def dev(dx, dz):
        return (chip(dx, dz) * 2 + c, j)

    loads = [
        pltpu.make_async_copy(w_h, w_own, in_sem.at[0]),
        pltpu.make_async_copy(acts_h, acts, in_sem.at[1]),
        pltpu.make_async_copy(pin_h, pin, in_sem.at[2]),
        pltpu.make_async_copy(pout_h, pout, in_sem.at[3]),
        pltpu.make_async_copy(pan_h, pan.at[c], in_sem.at[4]),
    ]

    def cot_load(s):
        rows = pl.ds(pl.multiple_of(lax.rem(j + s, 8) * PIECE, PIECE), PIECE)
        return pltpu.make_async_copy(cot_h.at[rows], cot.at[rows], cot_sem.at[s])

    for load in loads:
        load.start()
    cot_load(0).start()

    barrier = pltpu.get_barrier_semaphore()
    pl.semaphore_signal(barrier, inc=1, device_id=sib, device_id_type=MESH)

    @pl.loop(1, 8)
    def _(s):
        pl.semaphore_signal(barrier, inc=1, device_id=(i, lax.rem(j + s, 8)), device_id_type=MESH)

    @pl.loop(1, 16)
    def _(s):
        pl.semaphore_signal(
            barrier, inc=1, device_id=(lax.rem(q + s, 16) * 2 + c, j), device_id_type=MESH
        )

    eye = jnp.where(
        lax.broadcasted_iota(jnp.int32, (128, 128), 0) == lax.broadcasted_iota(jnp.int32, (128, 128), 1),
        1.0, 0.0,
    ).astype(BF16)
    loads[0].wait()
    wg[pl.ds(pl.multiple_of(q * 256 + c * 128, 128), 128), :] = dot(eye, w_own[...], 1, 1).astype(BF16)

    loads[1].wait()
    loads[2].wait()
    ip = dot(acts[...], pin[...], 1, 1)
    for to in range(8):
        block = ip[to * PIECE:(to + 1) * PIECE]
        in_send[to] = jnp.concatenate([block[:128], block[128:]], axis=1)
    loads[4].wait()
    pl.semaphore_wait(barrier, 23)

    def remote(src, dst, to, stage, s=0):
        return pltpu.make_async_remote_copy(
            src_ref=src, dst_ref=dst, send_sem=e_send.at[stage, s], recv_sem=e_recv.at[stage],
            device_id=to, device_id_type=MESH,
        )

    def copy_in(s):
        to = lax.rem(j + s, 8)
        return remote(in_send.at[to], in_recv.at[j], (i, to), 0, s)

    def copy_part(s):
        return remote(q_part, q_all.at[j], (i, lax.rem(j + s, 8)), 1, s)

    def copy_grads(s):
        to = lax.rem(q + s, 16)
        return remote(send2.at[to], g_all.at[c, q], (to * 2 + c, j), 2, s)

    def copy_pair():
        return remote(g_all.at[c], g_all.at[c], sib, 3)

    def copy_scores(s):
        to = lax.rem(q + s, 16)
        return remote(s_part.at[to], s_recv.at[q], (to * 2 + c, j), 4, s)

    def copy_panels():
        return remote(pan.at[c], pan.at[c], sib, 5)

    def exchange(n, copy_of):
        def go(s, _):
            copy_of(s).start()
            return 0
        lax.fori_loop(1, n, go, 0)

    def done_sending(n, copy_of):
        def go(s, _):
            copy_of(s).wait_send()
            return 0
        lax.fori_loop(1, n, go, 0)

    exchange(8, copy_in)
    copy_panels().start()

    def wrows(chip_index, core, half=None):
        start = chip_index * 256 + core * 128
        if half is None:
            return wg.at[pl.ds(pl.multiple_of(start, 128), 128)]
        return wg.at[pl.ds(pl.multiple_of(start + 64 * half, 64), 64)]

    sent = []

    def push(ref, to, recv):
        copy = pltpu.make_async_remote_copy(
            src_ref=ref, dst_ref=ref, send_sem=w_send.at[len(sent)], recv_sem=recv,
            device_id=to, device_id_type=MESH,
        )
        copy.start()
        sent.append(copy)

    def arrive(ref, sem):
        pltpu.make_async_copy(ref, ref, sem).wait()

    DZ = (0, -1, 1, 2)
    DX = (0, -1, 1, 2)

    def to_x(m):
        push(wrows(chip(0, DZ[m]), c), dev(1, 0), rx.at[m, 0])
        push(wrows(chip(0, DZ[m]), c), dev(-1, 0), rx.at[m, 1])

    def to_sib(m, k):
        push(wrows(chip(DX[k], DZ[m]), c), sib, rsib.at[m, k])

    push(wrows(q, c), dev(0, 1), rz.at[0])
    push(wrows(q, c), dev(0, -1), rz.at[1])
    to_x(0)
    to_sib(0, 0)

    def x_near(m):
        arrive(wrows(chip(-1, DZ[m]), c), rx.at[m, 0])
        push(wrows(chip(-1, DZ[m]), c, 0), dev(1, 0), rx.at[m, 2])
        to_sib(m, 1)
        arrive(wrows(chip(1, DZ[m]), c), rx.at[m, 1])
        push(wrows(chip(1, DZ[m]), c, 1), dev(-1, 0), rx.at[m, 3])
        to_sib(m, 2)

    def x_far(m):
        arrive(wrows(chip(2, DZ[m]), c, 0), rx.at[m, 2])
        arrive(wrows(chip(2, DZ[m]), c, 1), rx.at[m, 3])
        to_sib(m, 3)

    def z_near():
        arrive(wrows(chip(0, -1), c), rz.at[0])
        push(wrows(chip(0, -1), c, 0), dev(0, 1), rz.at[2])
        to_x(1)
        arrive(wrows(chip(0, 1), c), rz.at[1])
        push(wrows(chip(0, 1), c, 1), dev(0, -1), rz.at[3])
        to_x(2)
        to_sib(1, 0)
        to_sib(2, 0)

    def z_far():
        arrive(wrows(chip(0, 2), c, 0), rz.at[2])
        arrive(wrows(chip(0, 2), c, 1), rz.at[3])
        to_x(3)
        to_sib(3, 0)

    for step in range(1, 8):
        cot_load(step).start()

    loads[3].wait()
    row = lax.broadcasted_iota(jnp.int32, (64, 64), 0)
    col = lax.broadcasted_iota(jnp.int32, (64, 64), 1)
    even_odd = jnp.where(col == lax.rem(row, 32) * 2 + row // 32, 1.0, 0.0).astype(BF16)
    pout[...] = dot(even_odd, pout[...]).astype(BF16)
    cot_load(0).wait()
    op = dot(cot[pl.ds(pl.multiple_of(j * PIECE, PIECE), PIECE), :], pout[...], 1, 1)
    op_parts = two_parts(jnp.concatenate([op[:128], op[128:]], axis=1))

    def a_pass(first, second, mode):
        for m, k in (first, second):
            arrive(wrows(chip(DX[k], DZ[m]), 1 - c), rsib.at[m, k])
        ka = pl.ds(pl.multiple_of(chip(DX[first[1]], DZ[first[0]]) * 256, 256), 256)
        kb = pl.ds(pl.multiple_of(chip(DX[second[1]], DZ[second[0]]) * 256, 256), 256)
        new = dot(cot[:, ka], wg[ka, :]) + dot(cot[:, kb], wg[kb, :])
        if mode == 0:
            acc[...] = new
        elif mode == 1:
            acc[...] += new
        else:
            act_o[...] = (acc[...] + new).astype(BF16)

    x_near(0)
    for step in range(1, 8):
        cot_load(step).wait()
    a_pass((0, 0), (0, 1), 0)
    z_near()
    x_far(0)

    arrive(in_recv.at[pl.ds(0, 7)], e_recv.at[0])
    total = in_send[j]
    for step in range(1, 8):
        total = total + in_recv[lax.rem(j + step, 8)]
    part = dot(op_parts, two_parts(total), 0, 0)
    part = (part[:128, :128] + part[128:, 128:]) + (part[:128, 128:] + part[128:, :128])
    part = part[:64, :64] + part[64:, 64:]
    part = jnp.concatenate([part[:32], part[32:]], axis=1)
    q_part[...] = part
    exchange(8, copy_part)
    q_all[j] = part
    a_pass((0, 2), (1, 0), 1)
    z_far()
    a_pass((2, 0), (0, 3), 1)
    x_near(1)
    x_near(2)

    arrive(q_all.at[pl.ds(0, 7)], e_recv.at[1])
    for e in range(4):
        grads = (q_all[2 * e] + q_all[2 * e + 1]) * (1.0 / math.sqrt(LEN))
        for t in range(8):
            tiles_f[t, e * 4:e * 4 + 4, :] = grads[t * 4:t * 4 + 4]
    tiles[...] = tiles_f[...].astype(BF16)
    mine = tiles[j]
    for to in range(16):
        send2[to, 0] = tiles[to // 2]
        send2[to, 1] = mine
    exchange(16, copy_grads)
    g_all[c, q] = send2[q]
    a_pass((3, 0), (1, 1), 1)
    x_near(3)
    a_pass((1, 2), (2, 1), 1)
    x_far(1)
    x_far(2)
    a_pass((2, 2), (1, 3), 1)
    x_far(3)

    m = lax.broadcasted_iota(jnp.int32, (64, 256), 0)
    n = lax.broadcasted_iota(jnp.int32, (64, 256), 1)
    pick = [jnp.where(n == m * 4 + lax.rem(q, 2) * 2 + u, 1.0, 0.0).astype(BF16) for u in range(2)]
    arrive(pan.at[1 - c], e_recv.at[5])
    arrive(g_all.at[c, pl.ds(0, 15)], e_recv.at[2])
    copy_pair().start()
    own_tiles = g_all[c, :, 0].reshape(256, 128)
    score = dot(dot(pick[0], own_tiles).astype(BF16), pan[0])
    score += dot(dot(pick[1], own_tiles).astype(BF16), pan[1])
    for to in range(16):
        s_part[to] = score[to * 4:to * 4 + 4]
    exchange(16, copy_scores)
    a_pass((2, 3), (3, 1), 1)

    arrive(g_all.at[1 - c], e_recv.at[3])
    m = lax.broadcasted_iota(jnp.int32, (128, 512), 0)
    n = lax.broadcasted_iota(jnp.int32, (128, 512), 1)

    def select(r):
        return jnp.where(n == m * 4 + r, 1.0, 0.0).astype(BF16)

    row_tiles = g_all[:, :, 0].reshape(512, 128)
    col_tiles = g_all[:, :, 1].reshape(512, 128)
    g_rows = dot(select(lax.rem(i, 4)), row_tiles).astype(BF16)
    g_cols = jnp.concatenate([dot(select(r), col_tiles).astype(BF16) for r in range(4)], axis=1)
    fish_o[...] = dot(g_rows, g_cols, 0, 0) * (1.0 / 128)
    a_pass((3, 2), (3, 3), 2)

    arrive(s_recv.at[pl.ds(0, 15)], e_recv.at[4])
    total = s_part[q]
    for step in range(1, 16):
        total = total + s_recv[lax.rem(q + step, 16)]
    score_o[...] = total

    for copy in sent:
        copy.wait_send()
    done_sending(8, copy_in)
    done_sending(8, copy_part)
    done_sending(16, copy_grads)
    done_sending(16, copy_scores)
    copy_pair().wait_send()
    copy_panels().wait_send()


def per_device(acts, cotangent, out_weight, proj_in, proj_out, panels):
    rows, wide = cotangent.shape
    feats = acts.shape[1]
    any_spec = pl.BlockSpec(memory_space=pl.ANY)
    vmem_spec = pl.BlockSpec(memory_space=pltpu.VMEM)
    dma = pltpu.SemaphoreType.DMA
    operands = (acts, cotangent, out_weight, proj_in.T, proj_out.T, panels)
    operands = [pltpu.with_memory_space_constraint(a, pltpu.HBM) for a in operands]
    return pl.pallas_call(
        kernel,
        out_shape=(
            jax.ShapeDtypeStruct((rows, feats), BF16),
            jax.ShapeDtypeStruct((128, 512), F32),
            jax.ShapeDtypeStruct((4, 512), F32),
        ),
        in_specs=[any_spec] * 6,
        out_specs=(vmem_spec, vmem_spec, vmem_spec),
        scratch_shapes=[
            pltpu.VMEM((rows, feats), BF16),
            pltpu.VMEM((rows, wide), BF16),
            pltpu.VMEM((feats, 128), BF16),
            pltpu.VMEM((64, feats), BF16),
            pltpu.VMEM((64, wide), BF16),
            pltpu.VMEM((2, 128, 512), BF16),
            pltpu.VMEM((wide, feats), BF16),
            pltpu.VMEM((rows, feats), F32),
            pltpu.VMEM((8, 128, 128), F32),
            pltpu.VMEM((8, 128, 128), F32),
            pltpu.VMEM((32, 128), F32),
            pltpu.VMEM((8, 32, 128), F32),
            pltpu.VMEM((8, 16, 128), F32),
            pltpu.VMEM((8, 16, 128), BF16),
            pltpu.VMEM((16, 2, 16, 128), BF16),
            pltpu.VMEM((2, 16, 2, 16, 128), BF16),
            pltpu.VMEM((16, 4, 512), F32),
            pltpu.VMEM((16, 4, 512), F32),
            dma((5,)),
            dma((8,)),
            dma((36,)),
            dma((4,)),
            dma((4, 4)),
            dma((4, 4)),
            dma((6, 16)),
            dma((6,)),
        ],
        compiler_params=pltpu.CompilerParams(
            collective_id=0, has_side_effects=True, vmem_limit_bytes=40 * 1024 * 1024
        ),
        cost_estimate=pl.CostEstimate(
            flops=2 * rows * wide * (feats + 64), bytes_accessed=26 * 2**20, transcendentals=0
        ),
    )(*operands)


def solution(mesh):
    return jax.shard_map(
        per_device,
        mesh=mesh,
        in_specs=(
            P("dp", "fisher"),
            P("dp", None),
            P("fisher", "dp"),
            P("fisher", None),
            P(),
            P("dp", "fisher"),
        ),
        out_specs=(P("dp", "fisher"), P("dp", "fisher"), P("dp", "fisher")),
        check_vma=False,
    )
```

time: 59 us -> 53.8 us (0.912)
  Pallas kernels: 53.8 us -> 50.5 us
  local copies, waits for them, and re-layouts: 4.39 us -> 2.62 us
    pallas_call x1, Pallas kernels: 53.8 us -> 50.5 us  [per_device(): pl.pallas_call(kernel, out_shape=(jax.ShapeDtypeStruct((rows, feats), BF1...]
    unnamed x7 -> x3, local copies, waits for them, and re-layouts: 4.39 us -> 2.62 us
where the time goes in v3:
time: 53.8 us; the launch traced here: 53.7 us
  Pallas kernels  50.5 us (94%)
  local copies, waits for them, and re-layouts  2.62 us (5%)
  between operations  0.64 us (1%)
    pallas_call x1, Pallas kernels, per_device(): pl.pallas_call(kernel, out_shape=(jax.ShapeDtypeStruct((rows, feats), BF1...  50.5 us
    unnamed x3, local copies, waits for them, and re-layouts  2.62 us

profile of v3, /device:TPU:1, one launch (start us, length us, event | category | flops | bytes accessed | tf_op | source)
XLA Modules:
  0.0 53.7 jit_solution(1238160600509195294)
XLA Ops:
  0.6 50.5 %shard_map.85 = (bf16[2048,512]{1,0:T(8,128)(2,1)S(1)}, f32[128,512]{1,0:T(8,128)S(1)}, f32[4,512]{1,0:T(4,128)S(1)}) custom-call(bf16[2048,512]{1,0:T(8,128)(2,1)} %acts_h.1, bf16[2048,4096]{1,0:T(8,128)(2,1)} %cot_h.1, bf16[512,128]{1,0:T(8,128)(2,1)} %w_h.1, bf16[64,512]{1,0:T(8,128)(2,1)} %bitcast.3, bf16[64,4096]{1,0:T(8,128)(2,1)} %bitcast.2, ...), custom_call_target="tpu_custom_call" | custom-call | flops 9663676416 | bytes 27262976 | tf_op jit(solution)/shard_map/pallas_call | solution.py:323
  51.1 1.3 %copy.12 = bf16[2048,512]{1,0:T(8,128)(2,1)} copy(bf16[2048,512]{1,0:T(8,128)(2,1)S(1)} %get-tuple-element.6) | data formatting | bytes 4194304
  52.4 0.7 %copy.13 = f32[128,512]{1,0:T(8,128)} copy(f32[128,512]{1,0:T(8,128)S(1)} %get-tuple-element.7) | data formatting | bytes 524288
  53.1 0.6 %copy.14 = f32[4,512]{1,0:T(4,128)} copy(f32[4,512]{1,0:T(4,128)S(1)} %get-tuple-element.8) | data formatting | bytes 16384

commit v4 on v3

--- a/solution.py
+++ b/solution.py
@@ -30,7 +30,7 @@
     acts_h, cot_h, w_h, pin_h, pout_h, pan_h,
     act_o, fish_o, score_o,
     acts, cot, w_own, pin, pout, pan, wg, acc,
-    in_send, in_recv, q_part, q_all, tiles_f, tiles, send2, g_all, s_part, s_recv,
+    in_send, in_recv, q_part, q_all, tiles_f, tiles, g_rows_all, g_cols_all, s_part, s_recv,
     in_sem, cot_sem,
     w_send, rz, rx, rsib,
     e_send, e_recv,
@@ -90,7 +90,7 @@
     ip = dot(acts[...], pin[...], 1, 1)
     for to in range(8):
         block = ip[to * PIECE:(to + 1) * PIECE]
-        in_send[to] = jnp.concatenate([block[:128], block[128:]], axis=1)
+        in_send[to] = jnp.concatenate([block[:128], block[128:]], axis=1).astype(BF16)
     loads[4].wait()
     pl.semaphore_wait(barrier, 23)
 
@@ -109,10 +109,17 @@
 
     def copy_grads(s):
         to = lax.rem(q + s, 16)
-        return remote(send2.at[to], g_all.at[c, q], (to * 2 + c, j), 2, s)
+        return remote(tiles.at[to // 2], g_rows_all.at[c, q], (to * 2 + c, j), 2, s)
+
+    def copy_cols(s):
+        to = lax.rem(q + s, 16)
+        return remote(tiles.at[j], g_cols_all.at[c, q], (to * 2 + c, j), 6, s)
 
     def copy_pair():
-        return remote(g_all.at[c], g_all.at[c], sib, 3)
+        return remote(g_rows_all.at[c], g_rows_all.at[c], sib, 3)
+
+    def copy_pair_cols():
+        return remote(g_cols_all.at[c], g_cols_all.at[c], sib, 7)
 
     def copy_scores(s):
         to = lax.rem(q + s, 16)
@@ -158,45 +165,70 @@
     DZ = (0, -1, 1, 2)
     DX = (0, -1, 1, 2)
 
-    def to_x(m):
-        push(wrows(chip(0, DZ[m]), c), dev(1, 0), rx.at[m, 0])
-        push(wrows(chip(0, DZ[m]), c), dev(-1, 0), rx.at[m, 1])
+    def to_x(m, h):
+        block = wrows(chip(0, DZ[m]), c, h)
+        if h == 0:
+            push(block, dev(1, 0), rx.at[m, 0, h])
+            push(block, dev(-1, 0), rx.at[m, 1, h])
+        else:
+            push(block, dev(-1, 0), rx.at[m, 1, h])
+            push(block, dev(1, 0), rx.at[m, 0, h])
 
     def to_sib(m, k):
         push(wrows(chip(DX[k], DZ[m]), c), sib, rsib.at[m, k])
 
-    push(wrows(q, c), dev(0, 1), rz.at[0])
-    push(wrows(q, c), dev(0, -1), rz.at[1])
-    to_x(0)
+    push(wrows(q, c, 0), dev(0, 1), rz.at[0, 0])
+    push(wrows(q, c, 1), dev(0, -1), rz.at[1, 1])
+    push(wrows(q, c, 0), dev(1, 0), rx.at[0, 0, 0])
+    push(wrows(q, c, 1), dev(-1, 0), rx.at[0, 1, 1])
+    push(wrows(q, c, 1), dev(0, 1), rz.at[0, 1])
+    push(wrows(q, c, 0), dev(0, -1), rz.at[1, 0])
+    push(wrows(q, c, 1), dev(1, 0), rx.at[0, 0, 1])
+    push(wrows(q, c, 0), dev(-1, 0), rx.at[0, 1, 0])
     to_sib(0, 0)
 
-    def x_near(m):
-        arrive(wrows(chip(-1, DZ[m]), c), rx.at[m, 0])
-        push(wrows(chip(-1, DZ[m]), c, 0), dev(1, 0), rx.at[m, 2])
+    def x_up(m):
+        block = wrows(chip(-1, DZ[m]), c, 0)
+        arrive(block, rx.at[m, 0, 0])
+        push(block, dev(1, 0), rx.at[m, 2, 0])
+
+    def x_down(m):
+        block = wrows(chip(1, DZ[m]), c, 1)
+        arrive(block, rx.at[m, 1, 1])
+        push(block, dev(-1, 0), rx.at[m, 2, 1])
+
+    def x_rest(m):
+        arrive(wrows(chip(-1, DZ[m]), c, 1), rx.at[m, 0, 1])
         to_sib(m, 1)
-        arrive(wrows(chip(1, DZ[m]), c), rx.at[m, 1])
-        push(wrows(chip(1, DZ[m]), c, 1), dev(-1, 0), rx.at[m, 3])
+        arrive(wrows(chip(1, DZ[m]), c, 0), rx.at[m, 1, 0])
         to_sib(m, 2)
 
     def x_far(m):
-        arrive(wrows(chip(2, DZ[m]), c, 0), rx.at[m, 2])
-        arrive(wrows(chip(2, DZ[m]), c, 1), rx.at[m, 3])
+        arrive(wrows(chip(2, DZ[m]), c, 0), rx.at[m, 2, 0])
+        arrive(wrows(chip(2, DZ[m]), c, 1), rx.at[m, 2, 1])
         to_sib(m, 3)
 
-    def z_near():
-        arrive(wrows(chip(0, -1), c), rz.at[0])
-        push(wrows(chip(0, -1), c, 0), dev(0, 1), rz.at[2])
-        to_x(1)
-        arrive(wrows(chip(0, 1), c), rz.at[1])
-        push(wrows(chip(0, 1), c, 1), dev(0, -1), rz.at[3])
-        to_x(2)
+    def z_first():
+        arrive(wrows(chip(0, -1), c, 0), rz.at[0, 0])
+        push(wrows(chip(0, -1), c, 0), dev(0, 1), rz.at[2, 0])
+        to_x(1, 0)
+        arrive(wrows(chip(0, 1), c, 1), rz.at[1, 1])
+        push(wrows(chip(0, 1), c, 1), dev(0, -1), rz.at[2, 1])
+        to_x(2, 1)
+
+    def z_rest():
+        arrive(wrows(chip(0, -1), c, 1), rz.at[0, 1])
+        to_x(1, 1)
+        arrive(wrows(chip(0, 1), c, 0), rz.at[1, 0])
+        to_x(2, 0)
         to_sib(1, 0)
         to_sib(2, 0)
 
     def z_far():
-        arrive(wrows(chip(0, 2), c, 0), rz.at[2])
-        arrive(wrows(chip(0, 2), c, 1), rz.at[3])
-        to_x(3)
+        arrive(wrows(chip(0, 2), c, 0), rz.at[2, 0])
+        to_x(3, 0)
+        arrive(wrows(chip(0, 2), c, 1), rz.at[2, 1])
+        to_x(3, 1)
         to_sib(3, 0)
 
     for step in range(1, 8):
@@ -224,17 +256,15 @@
         else:
             act_o[...] = (acc[...] + new).astype(BF16)
 
-    x_near(0)
+    x_up(0)
+    x_down(0)
+    x_rest(0)
+    z_first()
+
+    arrive(in_recv.at[pl.ds(0, 7)], e_recv.at[0])
+    total = in_send[j].astype(F32)
     for step in range(1, 8):
-        cot_load(step).wait()
-    a_pass((0, 0), (0, 1), 0)
-    z_near()
-    x_far(0)
-
-    arrive(in_recv.at[pl.ds(0, 7)], e_recv.at[0])
-    total = in_send[j]
-    for step in range(1, 8):
-        total = total + in_recv[lax.rem(j + step, 8)]
+        total = total + in_recv[lax.rem(j + step, 8)].astype(F32)
     part = dot(op_parts, two_parts(total), 0, 0)
     part = (part[:128, :128] + part[128:, 128:]) + (part[:128, 128:] + part[128:, :128])
     part = part[:64, :64] + part[64:, 64:]
@@ -242,11 +272,14 @@
     q_part[...] = part
     exchange(8, copy_part)
     q_all[j] = part
+    for step in range(1, 8):
+        cot_load(step).wait()
+    a_pass((0, 0), (0, 1), 0)
+    x_far(0)
+    z_rest()
+    x_up(1)
+    x_down(2)
     a_pass((0, 2), (1, 0), 1)
-    z_far()
-    a_pass((2, 0), (0, 3), 1)
-    x_near(1)
-    x_near(2)
 
     arrive(q_all.at[pl.ds(0, 7)], e_recv.at[1])
     for e in range(4):
@@ -254,43 +287,52 @@
         for t in range(8):
             tiles_f[t, e * 4:e * 4 + 4, :] = grads[t * 4:t * 4 + 4]
     tiles[...] = tiles_f[...].astype(BF16)
-    mine = tiles[j]
-    for to in range(16):
-        send2[to, 0] = tiles[to // 2]
-        send2[to, 1] = mine
     exchange(16, copy_grads)
-    g_all[c, q] = send2[q]
+    exchange(16, copy_cols)
+    g_rows_all[c, q] = tiles[q // 2]
+    g_cols_all[c, q] = tiles[j]
+    z_far()
+    x_down(1)
+    x_up(2)
+    a_pass((2, 0), (0, 3), 1)
+    x_rest(1)
+    x_rest(2)
     a_pass((3, 0), (1, 1), 1)
-    x_near(3)
-    a_pass((1, 2), (2, 1), 1)
-    x_far(1)
-    x_far(2)
-    a_pass((2, 2), (1, 3), 1)
-    x_far(3)
 
     m = lax.broadcasted_iota(jnp.int32, (64, 256), 0)
     n = lax.broadcasted_iota(jnp.int32, (64, 256), 1)
     pick = [jnp.where(n == m * 4 + lax.rem(q, 2) * 2 + u, 1.0, 0.0).astype(BF16) for u in range(2)]
     arrive(pan.at[1 - c], e_recv.at[5])
-    arrive(g_all.at[c, pl.ds(0, 15)], e_recv.at[2])
-    copy_pair().start()
-    own_tiles = g_all[c, :, 0].reshape(256, 128)
+    arrive(g_rows_all.at[c, pl.ds(0, 15)], e_recv.at[2])
+    own_tiles = g_rows_all[c].reshape(256, 128)
     score = dot(dot(pick[0], own_tiles).astype(BF16), pan[0])
     score += dot(dot(pick[1], own_tiles).astype(BF16), pan[1])
     for to in range(16):
         s_part[to] = score[to * 4:to * 4 + 4]
     exchange(16, copy_scores)
+    x_up(3)
+    x_down(3)
+    copy_pair().start()
+    arrive(g_cols_all.at[c, pl.ds(0, 15)], e_recv.at[6])
+    copy_pair_cols().start()
+    x_far(1)
+    x_far(2)
+    a_pass((1, 2), (2, 1), 1)
+    x_rest(3)
+    a_pass((2, 2), (1, 3), 1)
+    x_far(3)
     a_pass((2, 3), (3, 1), 1)
 
-    arrive(g_all.at[1 - c], e_recv.at[3])
+    arrive(g_rows_all.at[1 - c], e_recv.at[3])
+    arrive(g_cols_all.at[1 - c], e_recv.at[7])
     m = lax.broadcasted_iota(jnp.int32, (128, 512), 0)
     n = lax.broadcasted_iota(jnp.int32, (128, 512), 1)
 
     def select(r):
         return jnp.where(n == m * 4 + r, 1.0, 0.0).astype(BF16)
 
-    row_tiles = g_all[:, :, 0].reshape(512, 128)
-    col_tiles = g_all[:, :, 1].reshape(512, 128)
+    row_tiles = g_rows_all[...].reshape(512, 128)
+    col_tiles = g_cols_all[...].reshape(512, 128)
     g_rows = dot(select(lax.rem(i, 4)), row_tiles).astype(BF16)
     g_cols = jnp.concatenate([dot(select(r), col_tiles).astype(BF16) for r in range(4)], axis=1)
     fish_o[...] = dot(g_rows, g_cols, 0, 0) * (1.0 / 128)
@@ -307,6 +349,8 @@
     done_sending(8, copy_in)
     done_sending(8, copy_part)
     done_sending(16, copy_grads)
+    done_sending(16, copy_cols)
+    copy_pair_cols().wait_send()
     done_sending(16, copy_scores)
     copy_pair().wait_send()
     copy_panels().wait_send()
@@ -338,24 +382,24 @@
             pltpu.VMEM((2, 128, 512), BF16),
             pltpu.VMEM((wide, feats), BF16),
             pltpu.VMEM((rows, feats), F32),
-            pltpu.VMEM((8, 128, 128), F32),
-            pltpu.VMEM((8, 128, 128), F32),
+            pltpu.VMEM((8, 128, 128), BF16),
+            pltpu.VMEM((8, 128, 128), BF16),
             pltpu.VMEM((32, 128), F32),
             pltpu.VMEM((8, 32, 128), F32),
             pltpu.VMEM((8, 16, 128), F32),
             pltpu.VMEM((8, 16, 128), BF16),
-            pltpu.VMEM((16, 2, 16, 128), BF16),
-            pltpu.VMEM((2, 16, 2, 16, 128), BF16),
+            pltpu.VMEM((2, 16, 16, 128), BF16),
+            pltpu.VMEM((2, 16, 16, 128), BF16),
             pltpu.VMEM((16, 4, 512), F32),
             pltpu.VMEM((16, 4, 512), F32),
             dma((5,)),
             dma((8,)),
-            dma((36,)),
-            dma((4,)),
+            dma((46,)),
+            dma((3, 2)),
+            dma((4, 3, 2)),
             dma((4, 4)),
-            dma((4, 4)),
-            dma((6, 16)),
-            dma((6,)),
+            dma((8, 16)),
+            dma((8,)),
         ],
         compiler_params=pltpu.CompilerParams(
             collective_id=0, has_side_effects=True, vmem_limit_bytes=40 * 1024 * 1024

time: 53.8 us -> 48.2 us (0.90)
  Pallas kernels: 50.5 us -> 44.9 us
    pallas_call x1, Pallas kernels: 50.5 us -> 44.9 us  [per_device(): pl.pallas_call(kernel, out_shape=(jax.ShapeDtypeStruct((rows, feats), BF1...]
where the time goes in v4:
time: 48.2 us; the launch traced here: 48.1 us
  Pallas kernels  44.9 us (93%)
  local copies, waits for them, and re-layouts  2.62 us (5%)
  between operations  0.64 us (1%)
    pallas_call x1, Pallas kernels, per_device(): pl.pallas_call(kernel, out_shape=(jax.ShapeDtypeStruct((rows, feats), BF1...  44.9 us
    unnamed x3, local copies, waits for them, and re-layouts  2.62 us

profile of v4, /device:TPU:1, one launch (start us, length us, event | category | flops | bytes accessed | tf_op | source)
XLA Modules:
  0.0 48.1 jit_solution(6062795204649042328)
XLA Ops:
  0.6 44.9 %shard_map.85 = (bf16[2048,512]{1,0:T(8,128)(2,1)S(1)}, f32[128,512]{1,0:T(8,128)S(1)}, f32[4,512]{1,0:T(4,128)S(1)}) custom-call(bf16[2048,512]{1,0:T(8,128)(2,1)} %acts_h.1, bf16[2048,4096]{1,0:T(8,128)(2,1)} %cot_h.1, bf16[512,128]{1,0:T(8,128)(2,1)} %w_h.1, bf16[64,512]{1,0:T(8,128)(2,1)} %bitcast.3, bf16[64,4096]{1,0:T(8,128)(2,1)} %bitcast.2, ...), custom_call_target="tpu_custom_call" | custom-call | flops 9663676416 | bytes 27262976 | tf_op jit(solution)/shard_map/pallas_call | solution.py:367
  45.5 1.3 %copy.12 = bf16[2048,512]{1,0:T(8,128)(2,1)} copy(bf16[2048,512]{1,0:T(8,128)(2,1)S(1)} %get-tuple-element.6) | data formatting | bytes 4194304
  46.8 0.7 %copy.13 = f32[128,512]{1,0:T(8,128)} copy(f32[128,512]{1,0:T(8,128)S(1)} %get-tuple-element.7) | data formatting | bytes 524288
  47.6 0.6 %copy.14 = f32[4,512]{1,0:T(4,128)} copy(f32[4,512]{1,0:T(4,128)S(1)} %get-tuple-element.8) | data formatting | bytes 16384

commit v5 on v4

--- a/solution.py
+++ b/solution.py
@@ -33,7 +33,7 @@
     in_send, in_recv, q_part, q_all, tiles_f, tiles, g_rows_all, g_cols_all, s_part, s_recv,
     in_sem, cot_sem,
     w_send, rz, rx, rsib,
-    e_send, e_recv,
+    e_send, e_recv, word,
 ):
     i = lax.axis_index("dp")
     j = lax.axis_index("fisher")
@@ -61,9 +61,8 @@
         rows = pl.ds(pl.multiple_of(lax.rem(j + s, 8) * PIECE, PIECE), PIECE)
         return pltpu.make_async_copy(cot_h.at[rows], cot.at[rows], cot_sem.at[s])
 
-    for load in loads:
+    for load in loads[:3]:
         load.start()
-    cot_load(0).start()
 
     barrier = pltpu.get_barrier_semaphore()
     pl.semaphore_signal(barrier, inc=1, device_id=sib, device_id_type=MESH)
@@ -72,11 +71,12 @@
     def _(s):
         pl.semaphore_signal(barrier, inc=1, device_id=(i, lax.rem(j + s, 8)), device_id_type=MESH)
 
-    @pl.loop(1, 16)
-    def _(s):
-        pl.semaphore_signal(
-            barrier, inc=1, device_id=(lax.rem(q + s, 16) * 2 + c, j), device_id_type=MESH
-        )
+    for near in (dev(1, 0), dev(-1, 0), dev(0, 1), dev(0, -1)):
+        pl.semaphore_signal(barrier, inc=1, device_id=near, device_id_type=MESH)
+
+    for load in loads[3:]:
+        load.start()
+    cot_load(0).start()
 
     eye = jnp.where(
         lax.broadcasted_iota(jnp.int32, (128, 128), 0) == lax.broadcasted_iota(jnp.int32, (128, 128), 1),
@@ -85,14 +85,16 @@
     loads[0].wait()
     wg[pl.ds(pl.multiple_of(q * 256 + c * 128, 128), 128), :] = dot(eye, w_own[...], 1, 1).astype(BF16)
 
-    loads[1].wait()
-    loads[2].wait()
-    ip = dot(acts[...], pin[...], 1, 1)
-    for to in range(8):
-        block = ip[to * PIECE:(to + 1) * PIECE]
-        in_send[to] = jnp.concatenate([block[:128], block[128:]], axis=1).astype(BF16)
-    loads[4].wait()
-    pl.semaphore_wait(barrier, 23)
+    pl.semaphore_wait(barrier, 12)
+
+    def tell(k):
+        for to in ((dev(1, 0), dev(-1, 0)) if k == 0 else (dev(0, 1), dev(0, -1))):
+            pl.semaphore_signal(word.at[k], inc=1, device_id=to, device_id_type=MESH)
+
+    def hear(k):
+        pl.semaphore_wait(word.at[k], 2)
+
+    tell(0)
 
     def remote(src, dst, to, stage, s=0):
         return pltpu.make_async_remote_copy(
@@ -139,9 +141,6 @@
             copy_of(s).wait_send()
             return 0
         lax.fori_loop(1, n, go, 0)
-
-    exchange(8, copy_in)
-    copy_panels().start()
 
     def wrows(chip_index, core, half=None):
         start = chip_index * 256 + core * 128
@@ -187,6 +186,16 @@
     push(wrows(q, c, 0), dev(-1, 0), rx.at[0, 1, 0])
     to_sib(0, 0)
 
+    loads[1].wait()
+    loads[2].wait()
+    ip = dot(acts[...], pin[...], 1, 1)
+    for to in range(8):
+        block = ip[to * PIECE:(to + 1) * PIECE]
+        in_send[to] = jnp.concatenate([block[:128], block[128:]], axis=1).astype(BF16)
+    exchange(8, copy_in)
+    loads[4].wait()
+    copy_panels().start()
+
     def x_up(m):
         block = wrows(chip(-1, DZ[m]), c, 0)
         arrive(block, rx.at[m, 0, 0])
@@ -233,6 +242,9 @@
 
     for step in range(1, 8):
         cot_load(step).start()
+
+    hear(0)
+    tell(1)
 
     loads[3].wait()
     row = lax.broadcasted_iota(jnp.int32, (64, 64), 0)
@@ -259,6 +271,8 @@
     x_up(0)
     x_down(0)
     x_rest(0)
+    hear(1)
+    tell(2)
     z_first()
 
     arrive(in_recv.at[pl.ds(0, 7)], e_recv.at[0])
@@ -274,9 +288,9 @@
     q_all[j] = part
     for step in range(1, 8):
         cot_load(step).wait()
+    z_rest()
     a_pass((0, 0), (0, 1), 0)
     x_far(0)
-    z_rest()
     x_up(1)
     x_down(2)
     a_pass((0, 2), (1, 0), 1)
@@ -287,6 +301,7 @@
         for t in range(8):
             tiles_f[t, e * 4:e * 4 + 4, :] = grads[t * 4:t * 4 + 4]
     tiles[...] = tiles_f[...].astype(BF16)
+    hear(2)
     exchange(16, copy_grads)
     exchange(16, copy_cols)
     g_rows_all[c, q] = tiles[q // 2]
@@ -356,6 +371,17 @@
     copy_panels().wait_send()
 
 
+def write_out(act, fish, score, act_o, fish_o, score_o, sem):
+    copies = [
+        pltpu.make_async_copy(src, dst, sem.at[n])
+        for n, (src, dst) in enumerate(((act, act_o), (fish, fish_o), (score, score_o)))
+    ]
+    for copy in copies:
+        copy.start()
+    for copy in copies:
+        copy.wait()
+
+
 def per_device(acts, cotangent, out_weight, proj_in, proj_out, panels):
     rows, wide = cotangent.shape
     feats = acts.shape[1]
@@ -364,13 +390,14 @@
     dma = pltpu.SemaphoreType.DMA
     operands = (acts, cotangent, out_weight, proj_in.T, proj_out.T, panels)
     operands = [pltpu.with_memory_space_constraint(a, pltpu.HBM) for a in operands]
-    return pl.pallas_call(
+    results = (
+        ((rows, feats), BF16),
+        ((128, 512), F32),
+        ((4, 512), F32),
+    )
+    held = pl.pallas_call(
         kernel,
-        out_shape=(
-            jax.ShapeDtypeStruct((rows, feats), BF16),
-            jax.ShapeDtypeStruct((128, 512), F32),
-            jax.ShapeDtypeStruct((4, 512), F32),
-        ),
+        out_shape=tuple(pltpu.VMEM(*r) for r in results),
         in_specs=[any_spec] * 6,
         out_specs=(vmem_spec, vmem_spec, vmem_spec),
         scratch_shapes=[
@@ -400,6 +427,7 @@
             dma((4, 4)),
             dma((8, 16)),
             dma((8,)),
+            pltpu.SemaphoreType.REGULAR((3,)),
         ],
         compiler_params=pltpu.CompilerParams(
             collective_id=0, has_side_effects=True, vmem_limit_bytes=40 * 1024 * 1024
@@ -408,6 +436,13 @@
             flops=2 * rows * wide * (feats + 64), bytes_accessed=26 * 2**20, transcendentals=0
         ),
     )(*operands)
+    return pl.pallas_call(
+        write_out,
+        out_shape=tuple(jax.ShapeDtypeStruct(*r) for r in results),
+        in_specs=[vmem_spec] * 3,
+        out_specs=(any_spec,) * 3,
+        scratch_shapes=[dma((3,))],
+    )(*(pltpu.with_memory_space_constraint(h, pltpu.VMEM) for h in held))
 
 
 def solution(mesh):

time: 48.2 us -> 45.5 us (0.944)
  local copies, waits for them, and re-layouts: 2.62 us -> 0 us
    unnamed x3 -> x0, local copies, waits for them, and re-layouts: 2.62 us -> none
    pallas_call x1 -> x2, Pallas kernels: 44.9 us -> 44.8 us  [the longest x1 43.4 us: per_device(): pl.pallas_call(kernel, out_shape=tuple((pltpu.VMEM(*r) for r in results))...]
where the time goes in v5:
time: 45.5 us
  Pallas kernels  44.8 us (98%)
  between operations  0.64 us (1%)
    pallas_call x1, Pallas kernels, per_device(): pl.pallas_call(kernel, out_shape=tuple((pltpu.VMEM(*r) for r in results))...  43.4 us
    pallas_call x1, Pallas kernels, per_device(): pl.pallas_call(write_out, out_shape=tuple((jax.ShapeDtypeStruct(*r) for r...  1.42 us

profile of v5, /device:TPU:1, one launch (start us, length us, event | category | flops | bytes accessed | tf_op | source)
XLA Modules:
  0.0 45.5 jit_solution(1428926433178024433)
XLA Ops:
  0.6 43.4 %shard_map.85 = (bf16[2048,512]{1,0:T(8,128)(2,1)S(1)}, f32[128,512]{1,0:T(8,128)S(1)}, f32[4,512]{1,0:T(4,128)S(1)}) custom-call(bf16[2048,512]{1,0:T(8,128)(2,1)} %acts_h.1, bf16[2048,4096]{1,0:T(8,128)(2,1)} %cot_h.1, bf16[512,128]{1,0:T(8,128)(2,1)} %w_h.1, bf16[64,512]{1,0:T(8,128)(2,1)} %bitcast.3, bf16[64,4096]{1,0:T(8,128)(2,1)} %bitcast.2, ...), custom_call_target="tpu_custom_call" | custom-call | flops 9663676416 | bytes 27262976 | tf_op jit(solution)/shard_map/pallas_call | solution.py:398
  44.0 1.4 %shard_map.86 = (bf16[2048,512]{1,0:T(8,128)(2,1)}, f32[128,512]{1,0:T(8,128)}, f32[4,512]{1,0:T(4,128)}) custom-call(bf16[2048,512]{1,0:T(8,128)(2,1)S(1)} %get-tuple-element.6.act, f32[128,512]{1,0:T(8,128)S(1)} %get-tuple-element.7.fish, f32[4,512]{1,0:T(4,128)S(1)} %get-tuple-element.8.score), custom_call_target="tpu_custom_call" | custom-call | tf_op jit(solution)/shard_map/pallas_call | solution.py:439

commit v6 on v5

--- a/solution.py
+++ b/solution.py
@@ -178,10 +178,10 @@
 
     push(wrows(q, c, 0), dev(0, 1), rz.at[0, 0])
     push(wrows(q, c, 1), dev(0, -1), rz.at[1, 1])
+    push(wrows(q, c, 1), dev(0, 1), rz.at[0, 1])
+    push(wrows(q, c, 0), dev(0, -1), rz.at[1, 0])
     push(wrows(q, c, 0), dev(1, 0), rx.at[0, 0, 0])
     push(wrows(q, c, 1), dev(-1, 0), rx.at[0, 1, 1])
-    push(wrows(q, c, 1), dev(0, 1), rz.at[0, 1])
-    push(wrows(q, c, 0), dev(0, -1), rz.at[1, 0])
     push(wrows(q, c, 1), dev(1, 0), rx.at[0, 0, 1])
     push(wrows(q, c, 0), dev(-1, 0), rx.at[0, 1, 0])
     to_sib(0, 0)
@@ -309,9 +309,11 @@
     z_far()
     x_down(1)
     x_up(2)
-    a_pass((2, 0), (0, 3), 1)
     x_rest(1)
     x_rest(2)
+    a_pass((2, 0), (0, 3), 1)
+    x_up(3)
+    x_down(3)
     a_pass((3, 0), (1, 1), 1)
 
     m = lax.broadcasted_iota(jnp.int32, (64, 256), 0)
@@ -325,8 +327,6 @@
     for to in range(16):
         s_part[to] = score[to * 4:to * 4 + 4]
     exchange(16, copy_scores)
-    x_up(3)
-    x_down(3)
     copy_pair().start()
     arrive(g_cols_all.at[c, pl.ds(0, 15)], e_recv.at[6])
     copy_pair_cols().start()
@@ -335,9 +335,6 @@
     a_pass((1, 2), (2, 1), 1)
     x_rest(3)
     a_pass((2, 2), (1, 3), 1)
-    x_far(3)
-    a_pass((2, 3), (3, 1), 1)
-
     arrive(g_rows_all.at[1 - c], e_recv.at[3])
     arrive(g_cols_all.at[1 - c], e_recv.at[7])
     m = lax.broadcasted_iota(jnp.int32, (128, 512), 0)
@@ -351,6 +348,10 @@
     g_rows = dot(select(lax.rem(i, 4)), row_tiles).astype(BF16)
     g_cols = jnp.concatenate([dot(select(r), col_tiles).astype(BF16) for r in range(4)], axis=1)
     fish_o[...] = dot(g_rows, g_cols, 0, 0) * (1.0 / 128)
+
+    x_far(3)
+    a_pass((2, 3), (3, 1), 1)
+
     a_pass((3, 2), (3, 3), 2)
 
     arrive(s_recv.at[pl.ds(0, 15)], e_recv.at[4])

time: 45.5 us -> 44.8 us (0.985)
  Pallas kernels: 44.8 us -> 44.1 us
    pallas_call x1, Pallas kernels: 43.4 us -> 42.6 us  [per_device(): pl.pallas_call(kernel, out_shape=tuple((pltpu.VMEM(*r) for r in results))...]
where the time goes in v6:
time: 44.8 us; the launch traced here: 44.7 us
  Pallas kernels  44.1 us (98%)
  between operations  0.64 us (1%)
    pallas_call x1, Pallas kernels, per_device(): pl.pallas_call(kernel, out_shape=tuple((pltpu.VMEM(*r) for r in results))...  42.6 us
    pallas_call x1, Pallas kernels, per_device(): pl.pallas_call(write_out, out_shape=tuple((jax.ShapeDtypeStruct(*r) for r...  1.42 us

profile of v6, /device:TPU:1, one launch (start us, length us, event | category | flops | bytes accessed | tf_op | source)
XLA Modules:
  0.0 44.7 jit_solution(5190569166757248711)
XLA Ops:
  0.6 42.6 %shard_map.85 = (bf16[2048,512]{1,0:T(8,128)(2,1)S(1)}, f32[128,512]{1,0:T(8,128)S(1)}, f32[4,512]{1,0:T(4,128)S(1)}) custom-call(bf16[2048,512]{1,0:T(8,128)(2,1)} %acts_h.1, bf16[2048,4096]{1,0:T(8,128)(2,1)} %cot_h.1, bf16[512,128]{1,0:T(8,128)(2,1)} %w_h.1, bf16[64,512]{1,0:T(8,128)(2,1)} %bitcast.3, bf16[64,4096]{1,0:T(8,128)(2,1)} %bitcast.2, ...), custom_call_target="tpu_custom_call" | custom-call | flops 9663676416 | bytes 27262976 | tf_op jit(solution)/shard_map/pallas_call | solution.py:399
  43.3 1.4 %shard_map.86 = (bf16[2048,512]{1,0:T(8,128)(2,1)}, f32[128,512]{1,0:T(8,128)}, f32[4,512]{1,0:T(4,128)}) custom-call(bf16[2048,512]{1,0:T(8,128)(2,1)S(1)} %get-tuple-element.6.act, f32[128,512]{1,0:T(8,128)S(1)} %get-tuple-element.7.fish, f32[4,512]{1,0:T(4,128)S(1)} %get-tuple-element.8.score), custom_call_target="tpu_custom_call" | custom-call | tf_op jit(solution)/shard_map/pallas_call | solution.py:440

commit v7 on v6

--- a/solution.py
+++ b/solution.py
@@ -354,12 +354,6 @@
 
     a_pass((3, 2), (3, 3), 2)
 
-    arrive(s_recv.at[pl.ds(0, 15)], e_recv.at[4])
-    total = s_part[q]
-    for step in range(1, 16):
-        total = total + s_recv[lax.rem(q + step, 16)]
-    score_o[...] = total
-
     for copy in sent:
         copy.wait_send()
     done_sending(8, copy_in)
@@ -367,9 +361,16 @@
     done_sending(16, copy_grads)
     done_sending(16, copy_cols)
     copy_pair_cols().wait_send()
-    done_sending(16, copy_scores)
     copy_pair().wait_send()
     copy_panels().wait_send()
+
+    arrive(s_recv.at[pl.ds(0, 15)], e_recv.at[4])
+    total = s_part[q]
+    for step in range(1, 16):
+        total = total + s_recv[lax.rem(q + step, 16)]
+    score_o[...] = total
+
+    done_sending(16, copy_scores)
 
 
 def write_out(act, fish, score, act_o, fish_o, score_o, sem):

time: 44.8 us -> 44.8 us (level)
  no operation moved by 1% of the time
where the time goes in v7:
time: 44.8 us; the launch traced here: 44.7 us
  Pallas kernels  44.1 us (98%)
  between operations  0.64 us (1%)
    pallas_call x1, Pallas kernels, per_device(): pl.pallas_call(kernel, out_shape=tuple((pltpu.VMEM(*r) for r in results))...  42.7 us
    pallas_call x1, Pallas kernels, per_device(): pl.pallas_call(write_out, out_shape=tuple((jax.ShapeDtypeStruct(*r) for r...  1.42 us

profile of v7, /device:TPU:1, one launch (start us, length us, event | category | flops | bytes accessed | tf_op | source)
XLA Modules:
  0.0 44.7 jit_solution(2254065739973905203)
XLA Ops:
  0.6 42.7 %shard_map.85 = (bf16[2048,512]{1,0:T(8,128)(2,1)S(1)}, f32[128,512]{1,0:T(8,128)S(1)}, f32[4,512]{1,0:T(4,128)S(1)}) custom-call(bf16[2048,512]{1,0:T(8,128)(2,1)} %acts_h.1, bf16[2048,4096]{1,0:T(8,128)(2,1)} %cot_h.1, bf16[512,128]{1,0:T(8,128)(2,1)} %w_h.1, bf16[64,512]{1,0:T(8,128)(2,1)} %bitcast.3, bf16[64,4096]{1,0:T(8,128)(2,1)} %bitcast.2, ...), custom_call_target="tpu_custom_call" | custom-call | flops 9663676416 | bytes 27262976 | tf_op jit(solution)/shard_map/pallas_call | solution.py:400
  43.3 1.4 %shard_map.86 = (bf16[2048,512]{1,0:T(8,128)(2,1)}, f32[128,512]{1,0:T(8,128)}, f32[4,512]{1,0:T(4,128)}) custom-call(bf16[2048,512]{1,0:T(8,128)(2,1)S(1)} %get-tuple-element.6.act, f32[128,512]{1,0:T(8,128)S(1)} %get-tuple-element.7.fish, f32[4,512]{1,0:T(4,128)S(1)} %get-tuple-element.8.score), custom_call_target="tpu_custom_call" | custom-call | tf_op jit(solution)/shard_map/pallas_call | solution.py:441
